TPU v7x, 32 devices: a whole 2x2x4 slice. The times are simulated.
32 devices in a mesh: dp: 8 (over z, x), section: 4 (over y, core).
Axes of the slice: x: 2, y: 2, z: 4, core: 2. Of those that a mesh axis runs over, the one named last changes fastest.
Arguments:
- tiles: bfloat16 [32, 128, 1536], P('dp'), may hold values from -6 to 6
- slide_ids: int32 [32, 128], P('dp'), may hold values from 0 to 2, never falling along the last dimension, each value on 1 to 64 neighbouring positions
- coords: int32 [2, 32, 128], P(None, 'dp'), may hold values from 0 to 255
- known: int32 [32, 3, 18], P('dp'), may hold values from 0 to 1
- labels: int32 [32, 3, 18], P('dp'), may hold values 0 or 1
- mats: float32 [4, 3, 768, 3072], P('section', None, 'dp')
- mats_m: float32 [4, 3, 768, 3072], P('section', None, 'dp'), may hold values from -5.722046e-06 to 5.722046e-06
- mats_v: float32 [4, 3, 768, 3072], P('section', None, 'dp'), may hold values from 4.455824e-12 to 1.7789412e-11
- gains: float32 [4, 2, 768], P('section')
- gains_m: float32 [4, 2, 768], P('section'), may hold values from -2.2888184e-05 to 2.2888184e-05
- gains_v: float32 [4, 2, 768], P('section'), may hold values from 7.129319e-11 to 2.846306e-10
- final_gain: float32 [768], P('section'), may hold values from 0.5 to 1.5
- fgain_m: float32 [768], P('section'), may hold values from -2.2888184e-05 to 2.2888184e-05
- fgain_v: float32 [768], P('section'), may hold values from 7.129319e-11 to 2.846306e-10
- w_in: float32 [1536, 768], P('section'), may hold values from -0.15625 to 0.15625
- win_m: float32 [1536, 768], P('section'), may hold values from -5.722046e-06 to 5.722046e-06
- win_v: float32 [1536, 768], P('section'), may hold values from 4.455824e-12 to 1.7789412e-11
- head: float32 [768, 18], P('section'), may hold values from -0.21875 to 0.21875
- head_m: float32 [768, 18], P('section'), may hold values from -5.722046e-06 to 5.722046e-06
- head_v: float32 [768, 18], P('section'), may hold values from 4.455824e-12 to 1.7789412e-11
Outputs:
- grad_norm: float32 [], replicated
- loss_sum: float32 [], replicated
- known_count: float32 [], replicated
- mats_m_new: float32 [4, 3, 768, 3072], P('section', None, 'dp')
- mats_v_new: float32 [4, 3, 768, 3072], P('section', None, 'dp')
- mats_new: float32 [4, 3, 768, 3072], P('section', None, 'dp')
- gains_m_new: float32 [4, 2, 768], P('section')
- gains_v_new: float32 [4, 2, 768], P('section')
- gains_new: float32 [4, 2, 768], P('section')
- fgain_m_new: float32 [768], P('section')
- fgain_v_new: float32 [768], P('section')
- fgain_new: float32 [768], P('section')
- win_m_new: float32 [1536, 768], P('section')
- win_v_new: float32 [1536, 768], P('section')
- win_new: float32 [1536, 768], P('section')
- head_m_new: float32 [768, 18], P('section')
- head_v_new: float32 [768, 18], P('section')
- head_new: float32 [768, 18], P('section')
Inputs may be any that keep to these rules, and one draw needn't show every extreme that they name: `slide_ids`: within a pack slide numbers never fall; each of the 3 slides has 1 to 64 tiles.
All inputs are finite; a program needn't handle non-finite values. No bound on the sum of `labels` on one device may be relied on, other than what follows from the above.
Results may differ from a plain program's by a relative error of at most 0.015.
Values may be sent and summed in bfloat16 or wider, within the bound.
No kernel may reach another device: no remote copies, remote signals or barrier semaphores. Data moves between devices by JAX's collectives and lax.ppermute only.
A program may use at most 576 MiB of HBM per device.

v0:
```python
import jax
import jax.numpy as jnp
from jax import lax
from jax.sharding import PartitionSpec as P

HEADS = 16
STEP = 10


EPS_NORM = 1e-05
CLIP = 0.05
BETA_ONE = 0.9
BETA_TWO = 0.95
ADAM_EPS = 1e-08
RATE = 0.06
RATE_GAIN = 1.0
DECAY = 0.1
RATIOS = (1, 2, 4, 8, 16)


def shifted(block, axis, distance):
    devices = range(lax.axis_size(axis))
    route = [(i - distance, i) for i in devices if i - distance in devices]
    return lax.ppermute(block, axis, route)


def layer_norm(value, gain):
    mean = jnp.mean(value, -1, keepdims=True)
    centred = value - mean
    var = jnp.mean(centred * centred, -1, keepdims=True)
    return centred * lax.rsqrt(var + EPS_NORM) * gain


def inner(left, right):
    return lax.dot_general(
        left, right, (((0,), (0,)), ((), ())), preferred_element_type=jnp.float32
    )


def against(left, right):
    return lax.dot_general(
        left, right, (((1,), (1,)), ((), ())), preferred_element_type=jnp.float32
    )


def position_table(coord, width):
    quarter = width // 4
    freq = jnp.exp(-jnp.log(10000.0) * jnp.arange(quarter, dtype=jnp.float32) / quarter)
    along = coord[0].astype(jnp.float32)[:, None] * freq
    across = coord[1].astype(jnp.float32)[:, None] * freq
    return jnp.concatenate(
        [jnp.sin(along), jnp.cos(along), jnp.sin(across), jnp.cos(across)], axis=1
    )


def score_bias(slide_row, heads):
    tok = slide_row.shape[0]
    place = jnp.arange(tok, dtype=jnp.int32)
    head_idx = jnp.arange(heads, dtype=jnp.int32)
    mult = jnp.zeros((heads, tok, tok), jnp.float32)
    for ratio in RATIOS:
        hit = (place[None, :] % ratio == head_idx[:, None] % ratio).astype(jnp.float32)
        mult = mult + hit[:, :, None] * hit[:, None, :]
    same = slide_row[:, None] == slide_row[None, :]
    return jnp.where(same[None], jnp.log(mult), -1000000000.0)


def split_heads(qkv, heads):
    tok, triple = qkv.shape
    width = triple // 3
    size = width // heads
    return (
        qkv[:, :width].reshape(tok, heads, size),
        qkv[:, width : 2 * width].reshape(tok, heads, size),
        qkv[:, 2 * width :].reshape(tok, heads, size),
    )


def layer_forward(x, wide, gain, bias, heads):
    tok, width = x.shape
    scale = (width // heads) ** (-0.5)
    a_low = layer_norm(x, gain[0]).astype(jnp.bfloat16)
    qkv = jnp.dot(a_low, wide[0][:, : 3 * width], preferred_element_type=jnp.float32).astype(
        jnp.bfloat16
    )
    query, keys, vals = split_heads(qkv, heads)
    scores = (
        jnp.einsum("thd,shd->hts", query, keys, preferred_element_type=jnp.float32) * scale + bias
    )
    lse = jax.nn.logsumexp(scores, axis=-1)
    prob = jnp.exp(scores - lse[..., None]).astype(jnp.bfloat16)
    attended = (
        jnp.einsum("hts,shd->thd", prob, vals, preferred_element_type=jnp.float32)
        .reshape(tok, width)
        .astype(jnp.bfloat16)
    )
    middle = x + jnp.dot(attended, wide[0][:, 3 * width :], preferred_element_type=jnp.float32)
    b_low = layer_norm(middle, gain[1]).astype(jnp.bfloat16)
    upper = jnp.dot(b_low, wide[1], preferred_element_type=jnp.float32)
    hidden = jax.nn.gelu(upper).astype(jnp.bfloat16)
    out = middle + against(hidden, wide[2])
    return (a_low, qkv, lse, attended, middle, b_low, upper, hidden, out)


def layer_backward(x, record, dout, wide, gain, bias, heads):
    a_low, qkv, lse, attended, middle, b_low, upper, hidden, out = record
    tok, width = x.shape
    scale = (width // heads) ** (-0.5)
    d_branch = dout.astype(jnp.bfloat16)
    grad_down = inner(d_branch, hidden)
    d_hidden = jnp.dot(d_branch, wide[2], preferred_element_type=jnp.float32)
    d_upper = jax.vjp(jax.nn.gelu, upper)[1](d_hidden)[0].astype(jnp.bfloat16)
    grad_up = inner(b_low, d_upper)
    d_b = against(d_upper, wide[1])
    back_mid = jax.vjp(layer_norm, middle, gain[1])[1](d_b)
    d_middle = dout + back_mid[0]
    d_attn_out = d_middle.astype(jnp.bfloat16)
    grad_out = inner(attended, d_attn_out)
    d_att = (
        against(d_attn_out, wide[0][:, 3 * width :])
        .astype(jnp.bfloat16)
        .reshape(tok, heads, width // heads)
    )
    query, keys, vals = split_heads(qkv, heads)
    scores = (
        jnp.einsum("thd,shd->hts", query, keys, preferred_element_type=jnp.float32) * scale + bias
    )
    prob = jnp.exp(scores - lse[..., None])
    d_prob = jnp.einsum("thd,shd->hts", d_att, vals, preferred_element_type=jnp.float32)
    d_vals = jnp.einsum(
        "hts,thd->shd", prob.astype(jnp.bfloat16), d_att, preferred_element_type=jnp.float32
    )
    d_scores = (prob * (d_prob - jnp.sum(d_prob * prob, -1, keepdims=True))).astype(jnp.bfloat16)
    d_query = jnp.einsum("hts,shd->thd", d_scores, keys, preferred_element_type=jnp.float32) * scale
    d_keys = jnp.einsum("hts,thd->shd", d_scores, query, preferred_element_type=jnp.float32) * scale
    d_qkv = jnp.concatenate(
        [d_query.reshape(tok, width), d_keys.reshape(tok, width), d_vals.reshape(tok, width)],
        axis=1,
    ).astype(jnp.bfloat16)
    grad_qkv = inner(a_low, d_qkv)
    d_a = against(d_qkv, wide[0][:, : 3 * width])
    back_front = jax.vjp(layer_norm, x, gain[0])[1](d_a)
    d_x = d_middle + back_front[0]
    grad_wide = jnp.stack([jnp.concatenate([grad_qkv, grad_out], axis=1), grad_up, grad_down])
    grad_gain = jnp.stack([back_front[1], back_mid[1]])
    return (d_x, grad_wide, grad_gain)


def head_step(out, slide_row, known_row, label_row, fgain, head_low, count):
    slides = known_row.shape[0]
    member = (slide_row[None, :] == jnp.arange(slides, dtype=jnp.int32)[:, None]).astype(
        jnp.float32
    )
    length = jnp.sum(member, 1, keepdims=True)
    pooled = (
        jnp.dot(member, out, precision=lax.Precision.HIGHEST, preferred_element_type=jnp.float32)
        / length
    )
    normed, norm_pull = jax.vjp(layer_norm, pooled, fgain)
    normed_low = normed.astype(jnp.bfloat16)
    logits = jnp.dot(normed_low, head_low, preferred_element_type=jnp.float32)
    terms = known_row * (jnp.logaddexp(0.0, logits) - label_row * logits)
    d_logits = (known_row * (jax.nn.sigmoid(logits) - label_row) / count).astype(jnp.bfloat16)
    grad_head = inner(normed_low, d_logits)
    d_normed = against(d_logits, head_low)
    d_pooled, grad_fgain = norm_pull(d_normed)
    d_out = inner(member, d_pooled / length)
    return (jnp.sum(terms), d_out, grad_head, grad_fgain)


def store(buffer, value, pick, valid):
    old = lax.dynamic_index_in_dim(buffer, pick, 0, keepdims=False)
    return lax.dynamic_update_index_in_dim(buffer, jnp.where(valid, value, old), pick, 0)


def fetch(buffer, pick):
    return lax.dynamic_index_in_dim(buffer, pick, 0, keepdims=False)


def adam(weight, grad, first, second, rate, decay):
    first = BETA_ONE * first + (1.0 - BETA_ONE) * grad
    second = BETA_TWO * second + (1.0 - BETA_TWO) * grad * grad
    mhat = first / (1.0 - BETA_ONE**STEP)
    vhat = second / (1.0 - BETA_TWO**STEP)
    return (first, second, weight - rate * (mhat / (jnp.sqrt(vhat) + ADAM_EPS) + decay * weight))


def per_device(
    tiles,
    slide_ids,
    coords,
    known,
    labels,
    mats,
    mats_m,
    mats_v,
    gains,
    gains_m,
    gains_v,
    final_gain,
    fgain_m,
    fgain_v,
    w_in,
    win_m,
    win_v,
    head,
    head_m,
    head_v,
):
    sections = lax.axis_size("section")
    section = lax.axis_index("section")
    first_dp = (lax.axis_index("dp") == 0).astype(jnp.float32)
    micro, tok = slide_ids.shape
    heads = HEADS
    wide = lax.all_gather(mats.astype(jnp.bfloat16), "dp", axis=2, tiled=True)[0]
    full_in, full_head, full_fgain = (
        lax.all_gather(w_in.astype(jnp.bfloat16), "section", axis=0, tiled=True).astype(w_in.dtype),
        lax.all_gather(head.astype(jnp.bfloat16), "section", axis=0, tiled=True).astype(head.dtype),
        lax.all_gather(final_gain.astype(jnp.bfloat16), "section", axis=0, tiled=True).astype(
            final_gain.dtype
        ),
    )
    in_low = full_in.astype(jnp.bfloat16)
    head_low = full_head.astype(jnp.bfloat16)
    gain = gains[0]
    width = wide.shape[1]
    known_f = known.astype(jnp.float32)
    labels_f = labels.astype(jnp.float32)
    count = jnp.maximum(lax.psum(jnp.sum(known_f), "dp"), 1.0)
    ticks = micro + sections - 1
    inputs = jnp.zeros((micro, tok, width), jnp.float32)
    kept = None
    received = jnp.zeros((tok, width), jnp.bfloat16)
    for tick in range(ticks):
        index = tick - section
        valid = (index >= 0) & (index < micro)
        pick = jnp.clip(index, 0, micro - 1)
        tile = fetch(tiles, pick)
        coord = lax.dynamic_index_in_dim(coords, pick, 1, keepdims=False)
        embedded = lax.cond(
            section == 0,
            lambda: jnp.dot(tile, in_low, preferred_element_type=jnp.float32)
            + position_table(coord, width),
            lambda: jnp.zeros((tok, width), jnp.float32),
        )
        x = jnp.where(section == 0, embedded, received.astype(jnp.float32))
        bias = score_bias(fetch(slide_ids, pick), heads)
        record = layer_forward(x, wide, gain, bias, heads)
        inputs = store(inputs, x, pick, valid)
        if kept is None:
            kept = jax.tree.map(lambda v: jnp.zeros((micro,) + v.shape, v.dtype), record)
        kept = jax.tree.map(lambda buf, v: store(buf, v, pick, valid), kept, record)
        if tick + 1 < ticks:
            received = shifted(record[-1].astype(jnp.bfloat16), "section", 1)
    grad_wide = jnp.zeros((3, width, wide.shape[2]), jnp.float32)
    grad_gain = jnp.zeros(gain.shape, jnp.float32)
    grad_in = jnp.zeros(full_in.shape, jnp.float32)
    grad_head = jnp.zeros(full_head.shape, jnp.float32)
    grad_fgain = jnp.zeros(full_fgain.shape, jnp.float32)
    loss_local = jnp.zeros((), jnp.float32)
    last = (section == sections - 1).astype(jnp.float32)
    incoming = jnp.zeros((tok, width), jnp.bfloat16)
    for tick in range(ticks):
        index = tick - (sections - 1 - section)
        valid = (index >= 0) & (index < micro)
        pick = jnp.clip(index, 0, micro - 1)
        use = valid.astype(jnp.float32)
        x = fetch(inputs, pick)
        record = jax.tree.map(lambda buf: fetch(buf, pick), kept)
        slide_row = fetch(slide_ids, pick)
        bias = score_bias(slide_row, heads)
        part, d_head_out, g_head, g_fgain = head_step(
            record[-1],
            slide_row,
            fetch(known_f, pick),
            fetch(labels_f, pick),
            full_fgain,
            head_low,
            count,
        )
        dout = jnp.where(section == sections - 1, d_head_out, incoming.astype(jnp.float32))
        d_x, g_wide, g_gain = layer_backward(x, record, dout, wide, gain, bias, heads)
        loss_local = loss_local + use * last * part
        grad_head = grad_head + use * last * g_head
        grad_fgain = grad_fgain + use * last * g_fgain
        grad_gain = grad_gain + use * g_gain
        grad_wide = grad_wide + use * g_wide
        d_low = d_x.astype(jnp.bfloat16)
        tile = fetch(tiles, pick)
        grad_in = grad_in + use * lax.cond(
            section == 0, lambda: inner(tile, d_low), lambda: jnp.zeros(full_in.shape, jnp.float32)
        )
        if tick + 1 < ticks:
            incoming = shifted(d_low, "section", -1)
    shard_wide = lax.psum_scatter(grad_wide, "dp", scatter_dimension=1, tiled=True)
    shard_wide = shard_wide[None]
    sum_gain, sum_in, sum_head, sum_fgain = lax.psum(
        (grad_gain, grad_in, grad_head, grad_fgain), "dp"
    )
    part_in, part_head, part_fgain = (
        lax.psum_scatter(sum_in, "section", scatter_dimension=0, tiled=True),
        lax.psum_scatter(sum_head, "section", scatter_dimension=0, tiled=True),
        lax.psum_scatter(sum_fgain, "section", scatter_dimension=0, tiled=True),
    )
    squares = jnp.sum(shard_wide * shard_wide) + first_dp * (
        jnp.sum(sum_gain * sum_gain)
        + jnp.sum(part_in * part_in)
        + jnp.sum(part_head * part_head)
        + jnp.sum(part_fgain * part_fgain)
    )
    total_sq, loss_sum = lax.psum((squares, loss_local), ("dp", "section"))
    grad_norm = jnp.sqrt(total_sq)
    factor = CLIP / jnp.maximum(grad_norm, CLIP)
    mats_out = adam(mats, shard_wide * factor, mats_m, mats_v, RATE, DECAY)
    gains_out = adam(gains, sum_gain[None] * factor, gains_m, gains_v, RATE_GAIN, 0.0)
    fgain_out = adam(final_gain, part_fgain * factor, fgain_m, fgain_v, RATE_GAIN, 0.0)
    in_out = adam(w_in, part_in * factor, win_m, win_v, RATE, DECAY)
    head_out = adam(head, part_head * factor, head_m, head_v, RATE, DECAY)
    return (
        grad_norm,
        loss_sum,
        count,
        mats_out[0],
        mats_out[1],
        mats_out[2],
        gains_out[0],
        gains_out[1],
        gains_out[2],
        fgain_out[0],
        fgain_out[1],
        fgain_out[2],
        in_out[0],
        in_out[1],
        in_out[2],
        head_out[0],
        head_out[1],
        head_out[2],
    )


def solution(mesh):
    placed = (
        P("dp", None, None),
        P("dp", None),
        P(None, "dp", None),
        P("dp", None, None),
        P("dp", None, None),
        P("section", None, "dp", None),
        P("section", None, "dp", None),
        P("section", None, "dp", None),
        P("section", None, None),
        P("section", None, None),
        P("section", None, None),
        P("section"),
        P("section"),
        P("section"),
        P("section", None),
        P("section", None),
        P("section", None),
        P("section", None),
        P("section", None),
        P("section", None),
    )
    return jax.shard_map(
        per_device,
        mesh=mesh,
        in_specs=placed,
        out_specs=(
            P(),
            P(),
            P(),
            P("section", None, "dp", None),
            P("section", None, "dp", None),
            P("section", None, "dp", None),
            P("section", None, None),
            P("section", None, None),
            P("section", None, None),
            P("section"),
            P("section"),
            P("section"),
            P("section", None),
            P("section", None),
            P("section", None),
            P("section", None),
            P("section", None),
            P("section", None),
        ),
        check_vma=False,
    )
```

profile of v0, /device:TPU:0, one launch (start us, length us, event | category | flops | bytes accessed | tf_op | source)
XLA Modules:
  0.0 1652.6 jit_solution(8689703073089242152)
XLA Ops:
  14.2 23.7 %psum.49 = f32[]{:T(128)} all-reduce(f32[]{:T(128)} %convert_reduce_fusion.7), channel_id=1, replica_groups=mesh['dp'=8,'section'=4] {'dp'}, use_global_device_ids=true, to_apply=%region_60.61 | all-reduce | flops 1 | bytes 8 | tf_op jit(solution)/shard_map/psum | solution.py:229
  39.4 5.6 all-reduce
  45.1 5.2 all-gather
  90.8 144.6 %all-gather.6.cloned.1.call-done = bf16[1,3,768,3072]{3,2,1,0:T(8,128)(2,1)} async-done(((bf16[1,3,96,3072]{3,2,1,0:T(8,128)(2,1)}), bf16[1,3,768,3072]{3,2,1,0:T(8,128)(2,1)}) %all-gather.6.cloned.1.call-update) | async-done | bytes 14155792 | tf_op jit(solution)/shard_map/all_gather | solution.py:215
  530.5 5.1 multiply_reduce_fusion.23
  826.0 13.8 multiply_add_fusion
  871.2 6.1 convolution_bitcast_fusion.12
  877.6 5.0 convolution_bitcast_fusion.13
  889.1 8.7 maximum_bitcast_fusion
  903.8 5.0 convolution_bitcast_fusion.11
  908.7 6.1 convolution_bitcast_fusion.10
  914.8 8.7 maximum_bitcast_fusion.1
  929.5 5.1 convolution_bitcast_fusion.9
  934.6 6.1 convolution_bitcast_fusion.8
  940.7 8.7 maximum_bitcast_fusion.2
  955.4 5.3 convolution_bitcast_fusion.7
  960.7 6.1 convolution_bitcast_fusion.6
  966.7 8.9 maximum_bitcast_fusion.3
  986.5 6.1 convolution_bitcast_fusion.4
  992.7 8.8 maximum_bitcast_fusion.4
  1007.4 5.1 convolution_bitcast_fusion.3
  1012.5 6.0 convolution_bitcast_fusion.2
  1018.5 8.7 maximum_bitcast_fusion.5
  1033.6 5.0 convolution_bitcast_fusion.1
  1038.7 8.9 maximum_bitcast_fusion.6
  1047.5 6.1 convolution_bitcast_fusion
  1053.7 73.1 %fusion.82 = f32[3,768,3072]{2,1,0:T(8,128)} fusion(f32[1,768,3072]{2,1,0:T(8,128)} %convolution_bitcast_fusion.12, f32[1,768,3072]{2,1,0:T(8,128)} %convolution_bitcast_fusion.13, f32[1,768,3072]{2,1,0:T(8,128)} %maximum_bitcast_fusion, f32[1,768,3072]{2,1,0:T(8,128)} %convolution_bitcast_fusion.10, f32[1,768,3072]{2,1,0:T(8,128)} %convolution_bitcast_fusion.11, ...), kind=kLoop, calls=%fused_computation.139 | loop fusion | flops 191102976 | bytes 226492448 | tf_op jit(solution)/shard_map/add | solution.py:287
  1132.0 5.8 all-reduce.1
  1139.2 36.2 %all-reduce.3 = (f32[2,768]{1,0:T(2,128)S(1)}, f32[192,18]{0,1:T(8,128)S(1)}, f32[192]{0:T(256)S(1)}) all-reduce(f32[2,768]{1,0:T(2,128)S(1)} %fusion.477, f32[192,18]{0,1:T(8,128)S(1)} %copy.427, f32[192]{0:T(256)S(1)} %dynamic-slice.2), channel_id=1, replica_groups=mesh['dp'=8,'section'=4] {'dp'}, use_global_device_ids=true, to_apply=%region_170.171 | all-reduce | flops 5184 | bytes 41472 | tf_op jit(solution)/shard_map/psum | solution.py:297
  1182.0 402.4 %reduce-scatter.6.cloned.1.call-done = f32[3,96,3072]{2,1,0:T(8,128)} async-done(((f32[3,768,3072]{2,1,0:T(8,128)}), f32[3,96,3072]{2,1,0:T(8,128)}) %reduce-scatter.6.cloned.1.call-update) | async-done | bytes 3538960 | tf_op jit(solution)/shard_map/reduce_scatter | solution.py:295
  1588.6 39.5 %all-reduce.2 = (f32[]{:T(128)}, f32[]{:T(128)}) all-reduce(f32[]{:T(128)S(6)} %add.2107, f32[]{:T(128)S(6)} %add.2120), channel_id=1, replica_groups=mesh['dp'=8,'section'=4] {'dp','section'}, use_global_device_ids=true, to_apply=%region_204.205 | all-reduce | flops 2 | bytes 16 | tf_op jit(solution)/shard_map/psum | solution.py:311
  1635.9 7.4 multiply_subtract_fusion
  (1842 shorter events, 771.2 us)
Async XLA Ops:
  7.2 55.8 %all-gather.4.cloned.1.call-start = ((), (), s32[]{:S(2)}) async-start(), calls=%async_computation.3 | async-start | bytes 2949120 | tf_op jit(solution)/shard_map/all_gather | solution.py:217
  9.4 226.0 %all-gather.6.cloned.1.call-start = ((), (), s32[]{:S(2)}) async-start(), calls=%async_computation.4 | async-start | bytes 15925248 | tf_op jit(solution)/shard_map/all_gather | solution.py:215
  13.0 1040.6 %reduce-scatter.8.cloned.1.call-start = ((), (), s32[]{:S(2)}) async-start(), calls=%async_computation.6 | async-start | bytes 5898240 | tf_op jit(solution)/shard_map/reduce_scatter | solution.py:301
  66.3 182.8 %copy-start.7 = (f32[128,768]{1,0:T(8,128)}, f32[128,768]{1,0:T(8,128)S(1)}, u32[]{:S(2)}) copy-start(f32[128,768]{1,0:T(8,128)S(1)} %get-tuple-element.946) | copy-start | bytes 1179652
  90.5 147.7 %copy-start.440 = (f32[128]{0:T(128)}, f32[128]{0:T(128)S(1)}, u32[]{:S(2)}) copy-start(f32[128]{0:T(128)S(1)} %broadcast_multiply_fusion.34) | copy-start | bytes 1540
  90.7 147.5 %copy-start.535 = (f32[128]{0:T(128)}, f32[128]{0:T(128)S(1)}, u32[]{:S(2)}) copy-start(f32[128]{0:T(128)S(1)} %add_rsqrt_fusion.13) | copy-start | bytes 1540
  262.6 8.7 collective-permute-start
  299.7 14.7 collective-permute-start.1
  341.7 12.3 collective-permute-start.2
  381.4 12.3 collective-permute-start.3
  421.0 12.4 collective-permute-start.4
  460.8 12.1 collective-permute-start.5
  550.5 79.4 %collective-permute-start.6 = (bf16[128,768]{1,0:T(8,128)(2,1)}, bf16[128,768]{1,0:T(8,128)(2,1)}, u32[]{:S(2)}, u32[]{:S(2)}) collective-permute-start(bf16[128,768]{1,0:T(8,128)(2,1)} %add_convert_fusion.6), channel_id=1, source_target_pairs={{1,0},{2,1},{3,2},{5,4},{6,5},{7,6},{9,8},{10,9},{11,10},{13,12},{... | collective-permute-start | bytes 589832 | tf_op jit(solution)/shard_map/ppermute | solution.py:24
  655.8 3.3 collective-permute-start.7
  683.2 6.1 collective-permute-start.8
  713.3 7.0 collective-permute-start.9
  744.4 7.0 collective-permute-start.10
  776.1 22.1 %collective-permute-start.11 = (bf16[128,768]{1,0:T(8,128)(2,1)}, bf16[128,768]{1,0:T(8,128)(2,1)}, u32[]{:S(2)}, u32[]{:S(2)}) collective-permute-start(bf16[128,768]{1,0:T(8,128)(2,1)} %add_convert_fusion.1), channel_id=1, source_target_pairs={{1,0},{2,1},{3,2},{5,4},{6,5},{7,6},{9,8},{10,9},{11,10},{13,12},{... | collective-permute-start | bytes 589832 | tf_op jit(solution)/shard_map/ppermute | solution.py:24
  839.9 298.0 %reduce-scatter.10.cloned.1.call-start = ((), (), s32[]{:S(2)}) async-start(), calls=%async_computation.8 | async-start | bytes 491520
  888.8 288.3 %all-reduce.6.cloned.1.call-start = ((), (), s32[]{:S(2)}) async-start(), calls=%async_computation.7 | async-start | bytes 2359296 | tf_op jit(solution)/shard_map/psum | solution.py:297
  1053.7 530.8 %reduce-scatter.6.cloned.1.call-start = ((), (), s32[]{:S(2)}) async-start(), calls=%async_computation.5 | async-start | bytes 31850496 | tf_op jit(solution)/shard_map/reduce_scatter | solution.py:295
  1181.9 447.0 %copy-start.453 = (f32[192]{0:T(256)S(1)}, f32[192]{0:T(256)}, u32[]{:S(2)}) copy-start(f32[192]{0:T(256)} %param.59) | copy-start | bytes 2308
  1181.9 447.0 %copy-start.454 = (f32[192]{0:T(256)S(1)}, f32[192]{0:T(256)}, u32[]{:S(2)}) copy-start(f32[192]{0:T(256)} %param.61) | copy-start | bytes 2308
  1181.9 447.0 %copy-start.455 = (f32[192]{0:T(256)S(1)}, f32[192]{0:T(256)}, u32[]{:S(2)}) copy-start(f32[192]{0:T(256)} %param.60) | copy-start | bytes 2308
  1181.9 447.6 %copy-start.272 = (f32[1,2,768]{2,1,0:T(2,128)S(1)}, f32[1,2,768]{2,1,0:T(2,128)}, u32[]{:S(2)}) copy-start(f32[1,2,768]{2,1,0:T(2,128)} %param.56) | copy-start | bytes 18436
  1182.0 447.6 %copy-start.359 = (f32[1,2,768]{2,1,0:T(2,128)S(1)}, f32[1,2,768]{2,1,0:T(2,128)}, u32[]{:S(2)}) copy-start(f32[1,2,768]{2,1,0:T(2,128)} %param.58) | copy-start | bytes 18436
  1182.0 447.5 %copy-start.360 = (f32[1,2,768]{2,1,0:T(2,128)S(1)}, f32[1,2,768]{2,1,0:T(2,128)}, u32[]{:S(2)}) copy-start(f32[1,2,768]{2,1,0:T(2,128)} %param.57) | copy-start | bytes 18436
  1182.0 448.2 %copy-start.257 = (f32[192,18]{0,1:T(8,128)S(1)}, f32[192,18]{0,1:T(8,128)}, u32[]{:S(2)}) copy-start(f32[192,18]{0,1:T(8,128)} %param.65) | copy-start | bytes 41476
  1182.0 448.2 %copy-start.273 = (f32[192,18]{0,1:T(8,128)S(1)}, f32[192,18]{0,1:T(8,128)}, u32[]{:S(2)}) copy-start(f32[192,18]{0,1:T(8,128)} %param.67) | copy-start | bytes 41476
  1182.0 448.1 %copy-start.274 = (f32[192,18]{0,1:T(8,128)S(1)}, f32[192,18]{0,1:T(8,128)}, u32[]{:S(2)}) copy-start(f32[192,18]{0,1:T(8,128)} %param.66) | copy-start | bytes 41476
  1182.0 448.8 %copy-start.62 = (f32[384,768]{1,0:T(8,128)S(1)}, f32[384,768]{1,0:T(8,128)}, u32[]{:S(2)}) copy-start(f32[384,768]{1,0:T(8,128)} %param.62) | copy-start | bytes 3538948
  1182.0 448.8 %copy-start.63 = (f32[384,768]{1,0:T(8,128)S(1)}, f32[384,768]{1,0:T(8,128)}, u32[]{:S(2)}) copy-start(f32[384,768]{1,0:T(8,128)} %all-reduce.6.cloned.1.call-done) | copy-start | bytes 3538948
  (559 other events, 2871.2 us)
Sparse Core Ops, SparseCore 0:
  10.2 26.7 all-gather.3
  39.7 195.6 all-gather.5
  840.0 45.0 reduce-scatter.7
  888.9 19.4 reduce-scatter.9
  1053.8 77.4 all-reduce.5
  1135.1 449.3 reduce-scatter.5
where the time goes:
time: 1670 us; the launch traced here: 1650 us
  waiting for transfers between devices  562 us (34%)
  matrix products  444 us (27%)
  other arithmetic  269 us (16%)
  local copies, waits for them, and re-layouts  201 us (12%)
  blocking collectives  116 us (7%)
  between operations  34.6 us (2%)
  starting transfers between devices  24.2 us (1%)
    reduce_scatter x1, waiting for transfers between devices, per_device(): lax.psum_scatter(grad_wide, 'dp', scatter_dimension=1, tiled=True)  402 us
    dot_general x49, matrix products, inner(): lax.dot_general(left, right, (((0,), (0,)), ((), ())), preferred_element_...  155 us
    all_gather x1, waiting for transfers between devices, per_device(): lax.all_gather(mats.astype(jnp.bfloat16), 'dp', axis=2, tiled=True)[0]  145 us
    dot_general x35, matrix products, against(): lax.dot_general(left, right, (((1,), (1,)), ((), ())), preferred_element_...  113 us
    add x1, other arithmetic, per_device(): grad_wide = grad_wide + use * g_wide  73.1 us
    dynamic_slice x48, local copies, waits for them, and re-layouts, store(): old = lax.dynamic_index_in_dim(buffer, pick, 0, keepdims=False)  63.4 us
    another operation x7, other arithmetic, layer_backward(): jnp.stack([jnp.concatenate([grad_qkv, grad_out], axis=1), grad_up, grad_d...  61.3 us
    psum x1, blocking collectives, per_device(): total_sq, loss_sum = lax.psum((squares, loss_local), ('dp', 'section'))  39.5 us
  transfers between devices with their start and end apart: 18, of which 6 were waited for; matrix products, arithmetic and copies ran while one was open for 29% of the time, Pallas kernels for 0%

commit v1 on v0

v1 whole, which is shorter than its diff:
```python
import functools

import jax
import jax.numpy as jnp
from jax import lax
from jax.experimental import pallas as pl
from jax.experimental.pallas import tpu as pltpu
from jax.sharding import PartitionSpec as P

HEADS = 16
STEP = 10


EPS_NORM = 1e-05
CLIP = 0.05
BETA_ONE = 0.9
BETA_TWO = 0.95
ADAM_EPS = 1e-08
RATE = 0.06
RATE_GAIN = 1.0
DECAY = 0.1
RATIOS = (1, 2, 4, 8, 16)

def shifted(block, axis, distance):
    devices = range(lax.axis_size(axis))
    route = [(i - distance, i) for i in devices if i - distance in devices]
    return lax.ppermute(block, axis, route)


def inner(left, right):
    return lax.dot_general(
        left, right, (((0,), (0,)), ((), ())), preferred_element_type=jnp.float32
    )


def position_table(coord, width):
    quarter = width // 4
    freq = jnp.exp(-jnp.log(10000.0) * jnp.arange(quarter, dtype=jnp.float32) / quarter)
    along = coord[0].astype(jnp.float32)[:, None] * freq
    across = coord[1].astype(jnp.float32)[:, None] * freq
    return jnp.concatenate(
        [jnp.sin(along), jnp.cos(along), jnp.sin(across), jnp.cos(across)], axis=1
    )


def log_mult(heads, tok):
    place = jnp.arange(tok, dtype=jnp.int32)
    head_idx = jnp.arange(heads, dtype=jnp.int32)
    mult = jnp.zeros((heads, tok, tok), jnp.float32)
    for ratio in RATIOS:
        hit = (place[None, :] % ratio == head_idx[:, None] % ratio).astype(jnp.float32)
        mult = mult + hit[:, :, None] * hit[:, None, :]
    return jnp.log(mult)


NN = (((1,), (0,)), ((), ()))
NT = (((1,), (1,)), ((), ()))
TN = (((0,), (0,)), ((), ()))
LANES = 128
BF = jnp.bfloat16
F32 = jnp.float32


def mm(left, right, dims=NN):
    return lax.dot_general(left, right, dims, preferred_element_type=F32)


def norm_parts(value):
    mean = jnp.mean(value, -1, keepdims=True)
    centred = value - mean
    var = jnp.mean(centred * centred, -1, keepdims=True)
    inv = lax.rsqrt(var + EPS_NORM)
    return centred * inv, inv


def norm_back(dvalue, gain, hat, inv):
    dhat = dvalue * gain
    return inv * (
        dhat
        - jnp.mean(dhat, -1, keepdims=True)
        - hat * jnp.mean(dhat * hat, -1, keepdims=True)
    )


def window(head, size):
    low = head * size // LANES * LANES
    high = -(-(head + 1) * size // LANES) * LANES
    return low, high


def placed_rows(ref, head, size):
    low, high = window(head, size)
    before, after = head * size - low, high - (head + 1) * size
    tok = ref.shape[1]
    parts = [ref[head * size : (head + 1) * size, :]]
    if before:
        parts = [jnp.zeros((before, tok), ref.dtype)] + parts
    if after:
        parts = parts + [jnp.zeros((after, tok), ref.dtype)]
    return jnp.concatenate(parts, axis=0) if len(parts) > 1 else parts[0]


def same_slide(ids_ref, pick):
    tok = ids_ref.shape[1]
    row = jnp.broadcast_to(ids_ref[pl.ds(pick, 1), :].astype(F32), (tok, tok))
    return row, row.T


def forward_kernel(
    heads, slides, scal, ids, gain, fgain, head_w, known, label, count,
    x0_h, rc_h, lm_h, wa_h, w1_h, w2_h, *rest
):
    fresh = rest[0]
    n_buf = 13
    rest = rest[1:] if fresh else rest[1 + n_buf :]
    send_h = rest[0]
    (x_b, qkv_b, lse_b, att_b, mid_b, gp_b, hid_b, a_b, b_b, dl_b, nl_b, dlog_b, side_b) = rest[1 : 1 + n_buf]
    (x_v, lm_v, wa, w1, w2, qkv_v, lse_v, att_v, mid_v, gp_v, hid_v, a_v, b_v, o_v, send_v,
     q_t, v_t, o_t, pool_v, nl_v, dlog_v, side_v, sin, sout) = rest[1 + n_buf :]
    valid, pick, first, last = scal[0], scal[1], scal[2], scal[3]
    tok, width = x_v.shape
    size = width // heads
    scale = size ** (-0.5)

    @pl.when(valid == 1)
    def _():
        weights = [
            pltpu.make_async_copy(wa_h.at[:, : 3 * width], wa.at[:, : 3 * width], sin.at[1]),
            pltpu.make_async_copy(lm_h, lm_v, sin.at[2]),
            pltpu.make_async_copy(wa_h.at[:, 3 * width :], wa.at[:, 3 * width :], sin.at[3]),
            pltpu.make_async_copy(w1_h, w1, sin.at[4]),
            pltpu.make_async_copy(w2_h, w2, sin.at[5]),
        ]
        from_table = pltpu.make_async_copy(x0_h.at[pick], x_v, sin.at[0])
        from_wire = pltpu.make_async_copy(rc_h, x_v, sin.at[0])

        @pl.when(first == 1)
        def _():
            from_table.start()

        @pl.when(first != 1)
        def _():
            from_wire.start()

        for c in weights:
            c.start()
        outs = []

        def emit(src, dst):
            c = pltpu.make_async_copy(src, dst, sout.at[len(outs)])
            c.start()
            outs.append(c)

        row, col = same_slide(ids, pick)
        same = row == col

        @pl.when(first == 1)
        def _():
            from_table.wait()

        @pl.when(first != 1)
        def _():
            from_wire.wait()

        emit(x_v, x_b.at[pick])
        x = x_v[...].astype(F32)
        hat, _ = norm_parts(x)
        a_v[...] = (hat * gain[0:1, :]).astype(BF)
        emit(a_v, a_b.at[pick])
        weights[0].wait()
        qkv_v[...] = mm(a_v[...], wa[:, : 3 * width]).astype(BF)
        emit(qkv_v, qkv_b.at[pick])
        q_t[...] = qkv_v[:, :width].T
        v_t[...] = qkv_v[:, 2 * width :].T
        weights[1].wait()
        for h in range(heads):
            low, high = window(h, size)
            s = mm(qkv_v[:, width + low : width + high], placed_rows(q_t, h, size)) * scale
            s = s + jnp.where(same, lm_v[h], -1000000000.0)
            top = jnp.max(s, 0, keepdims=True)
            e = jnp.exp(s - top)
            total = jnp.sum(e, 0, keepdims=True)
            lse_v[h : h + 1, :] = top + jnp.log(total)
            o = mm(v_t[h * size : (h + 1) * size, :], e.astype(BF))
            o_t[h * size : (h + 1) * size, :] = o * (1.0 / total)
        att_v[...] = o_t[...].T.astype(BF)
        emit(lse_v, lse_b.at[pick])
        emit(att_v, att_b.at[pick])
        weights[2].wait()
        middle = x + mm(att_v[...], wa[:, 3 * width :])
        mid_v[...] = middle
        emit(mid_v, mid_b.at[pick])
        hat, _ = norm_parts(middle)
        b_v[...] = (hat * gain[1:2, :]).astype(BF)
        emit(b_v, b_b.at[pick])
        weights[3].wait()
        ff = w1.shape[1]
        part = ff // 4
        for j in range(4):
            cols = slice(j * part, (j + 1) * part)
            up = mm(b_v[...], w1[:, cols])
            square = up * up
            sig = 1.0 / (1.0 + jnp.exp(up * (-1.5957691216057308 - 0.07135481627159852 * square)))
            act = up * sig
            hid_v[:, cols] = act.astype(BF)
            slope = 1.5957691216057308 + 0.21406444881478 * square
            gp_v[:, cols] = sig + act * (1.0 - sig) * slope
        emit(gp_v, gp_b.at[pick])
        emit(hid_v, hid_b.at[pick])
        weights[4].wait()
        out = mid_v[...] + mm(hid_v[...], w2[...], NT)
        send_v[...] = out.astype(BF)
        emit(send_v, send_h)

        @pl.when(last == 1)
        def _():
            o_v[...] = out
            pool_v[...] = jnp.zeros_like(pool_v)
            inverse = []
            for s in range(slides):
                inside = (col == float(s)).astype(F32)
                inverse.append(1.0 / jnp.sum(inside, 0, keepdims=True))
                parts = []
                for j in range(width // LANES):
                    parts.append(
                        jnp.sum(o_v[:, j * LANES : (j + 1) * LANES] * inside, 0, keepdims=True) * inverse[s]
                    )
                pool_v[s : s + 1, :] = jnp.concatenate(parts, axis=1)
            hat, inv = norm_parts(pool_v[...])
            low_n = (hat * fgain[...]).astype(BF)
            nl_v[...] = low_n
            logits = mm(low_n, head_w[...])
            kn = known[pick]
            lb = label[pick]
            tail = jnp.exp(-jnp.abs(logits))
            soft = jnp.maximum(logits, 0.0) + jnp.log(1.0 + tail)
            terms = kn * (soft - lb * logits)
            gate = jnp.where(logits >= 0.0, 1.0, tail) / (1.0 + tail)
            dlog = (kn * (gate - lb) / count[0, 0]).astype(BF)
            dlog_v[...] = dlog
            d_n = mm(dlog, head_w[...], NT)
            side_v[...] = jnp.zeros_like(side_v)
            side_v[0:1, :] = jnp.sum(d_n * hat, 0, keepdims=True)
            side_v[1:2, 0:LANES] = jnp.sum(terms, 0, keepdims=True)
            d_pool = norm_back(d_n, fgain[...], hat, inv)
            pool_v[...] = d_pool
            for j in range(width // LANES):
                lanes = slice(j * LANES, (j + 1) * LANES)
                acc = jnp.zeros((tok, LANES), F32)
                for s in range(slides):
                    acc = acc + jnp.where(col == float(s), pool_v[s : s + 1, lanes] * inverse[s], 0.0)
                o_v[:, lanes] = acc
            tails = [
                pltpu.make_async_copy(o_v, dl_b.at[pick], sin.at[0]),
                pltpu.make_async_copy(nl_v, nl_b.at[pick], sin.at[1]),
                pltpu.make_async_copy(dlog_v, dlog_b.at[pick], sin.at[2]),
                pltpu.make_async_copy(side_v, side_b.at[pick], sin.at[3]),
            ]
            for c in tails:
                c.start()
            for c in tails:
                c.wait()

        for c in outs:
            c.wait()


def backward_kernel(
    heads, scal, ids, gain, rc_h, dl_b, lm_h, wa_h, w1_h, w2_h,
    x_b, qkv_b, lse_b, mid_b, gp_b, *rest
):
    fresh = rest[0]
    n_buf = 5
    rest = rest[1:] if fresh else rest[1 + n_buf :]
    send_h = rest[0]
    (dbr_b, dup_b, dat_b, dqkv_b, gg_b) = rest[1 : 1 + n_buf]
    (rc_v, dl_v, lm_v, wa, w1, w2, x_v, qkv_v, lse_v, mid_v, gp_v,
     dbr_v, dup_v, dat_v, dqkv_v, gg_v, send_v, dm_v, q_t, k_t, do_v, do_t, dq_t, p_v, ds_v, sin, sout) = rest[1 + n_buf :]
    valid, pick, last = scal[0], scal[1], scal[3]
    tok, width = x_v.shape
    size = width // heads
    scale = size ** (-0.5)
    per = 8

    @pl.when(valid == 1)
    def _():
        from_wire = pltpu.make_async_copy(rc_h, rc_v, sin.at[0])
        from_head = pltpu.make_async_copy(dl_b.at[pick], dl_v, sin.at[0])

        @pl.when(last == 1)
        def _():
            from_head.start()

        @pl.when(last != 1)
        def _():
            from_wire.start()

        loads = [
            pltpu.make_async_copy(w2_h, w2, sin.at[1]),
            pltpu.make_async_copy(gp_b.at[pick], gp_v, sin.at[2]),
            pltpu.make_async_copy(w1_h, w1, sin.at[3]),
            pltpu.make_async_copy(mid_b.at[pick], mid_v, sin.at[4]),
            pltpu.make_async_copy(qkv_b.at[pick], qkv_v, sin.at[5]),
            pltpu.make_async_copy(wa_h.at[:, 3 * width :], wa.at[:, 3 * width :], sin.at[6]),
            pltpu.make_async_copy(lse_b.at[pick], lse_v, sin.at[7]),
            pltpu.make_async_copy(lm_h, lm_v, sin.at[8]),
            pltpu.make_async_copy(wa_h.at[:, : 3 * width], wa.at[:, : 3 * width], sin.at[9]),
            pltpu.make_async_copy(x_b.at[pick], x_v, sin.at[10]),
        ]
        for c in loads:
            c.start()
        outs = []

        def emit(src, dst):
            c = pltpu.make_async_copy(src, dst, sout.at[len(outs)])
            c.start()
            outs.append(c)

        row, col = same_slide(ids, pick)
        same = row == col

        @pl.when(last == 1)
        def _():
            from_head.wait()

        @pl.when(last != 1)
        def _():
            from_wire.wait()
            dl_v[...] = rc_v[...].astype(F32)

        dbr_v[...] = dl_v[...].astype(BF)
        emit(dbr_v, dbr_b.at[pick])
        loads[0].wait()
        loads[1].wait()
        ff = w1.shape[1]
        part = ff // 4
        for j in range(4):
            cols = slice(j * part, (j + 1) * part)
            dup_v[:, cols] = (mm(dbr_v[...], w2[:, cols]) * gp_v[:, cols]).astype(BF)
        emit(dup_v, dup_b.at[pick])
        loads[2].wait()
        d_b = mm(dup_v[...], w1[...], NT)
        loads[3].wait()
        hat, inv = norm_parts(mid_v[...])
        gg_v[1:2, :] = jnp.sum(d_b * hat, 0, keepdims=True)
        d_mid = dl_v[...] + norm_back(d_b, gain[1:2, :], hat, inv)
        dm_v[...] = d_mid
        dat_v[...] = d_mid.astype(BF)
        emit(dat_v, dat_b.at[pick])
        loads[4].wait()
        q_t[...] = qkv_v[:, :width].T
        k_t[...] = qkv_v[:, width : 2 * width].T
        loads[5].wait()
        do_v[...] = mm(dat_v[...], wa[:, 3 * width :], NT).astype(BF)
        do_t[...] = do_v[...].T
        loads[6].wait()
        loads[7].wait()
        lane = lax.broadcasted_iota(jnp.int32, (tok, LANES), 1)
        for group in range(heads // per):
            for i in range(per):
                h = group * per + i
                low, high = window(h, size)
                s = mm(qkv_v[:, width + low : width + high], placed_rows(q_t, h, size)) * scale
                s = s + jnp.where(same, lm_v[h], -1000000000.0)
                p = jnp.exp(s - lse_v[h : h + 1, :])
                dp = mm(qkv_v[:, 2 * width + low : 2 * width + high], placed_rows(do_t, h, size))
                inner_sum = jnp.sum(dp * p, 0, keepdims=True)
                ds = (p * (dp - inner_sum)).astype(BF)
                p_v[:, i * tok : (i + 1) * tok] = p.astype(BF)
                ds_v[:, i * tok : (i + 1) * tok] = ds
                dq_t[h * size : (h + 1) * size, :] = mm(k_t[h * size : (h + 1) * size, :], ds) * scale
            base = group * per * size
            for block in range(base // LANES, (base + per * size) // LANES):
                left = block * LANES
                inside = [
                    i for i in range(per)
                    if (group * per + i) * size < left + LANES and (group * per + i + 1) * size > left
                ]
                spans = slice(inside[0] * tok, (inside[-1] + 1) * tok)
                q_parts, o_parts = [], []
                for i in inside:
                    start = (group * per + i) * size - left
                    keep = (lane >= start) & (lane < start + size)
                    q_parts.append(jnp.where(keep, qkv_v[:, left : left + LANES], jnp.zeros((), BF)))
                    o_parts.append(jnp.where(keep, do_v[:, left : left + LANES], jnp.zeros((), BF)))
                dk = mm(ds_v[:, spans], jnp.concatenate(q_parts, axis=0)) * scale
                dv = mm(p_v[:, spans], jnp.concatenate(o_parts, axis=0))
                dqkv_v[:, width + left : width + left + LANES] = dk.astype(BF)
                dqkv_v[:, 2 * width + left : 2 * width + left + LANES] = dv.astype(BF)
        dqkv_v[:, :width] = dq_t[...].T.astype(BF)
        emit(dqkv_v, dqkv_b.at[pick])
        loads[8].wait()
        d_a = mm(dqkv_v[...], wa[:, : 3 * width], NT)
        loads[9].wait()
        hat, inv = norm_parts(x_v[...].astype(F32))
        gg_v[0:1, :] = jnp.sum(d_a * hat, 0, keepdims=True)
        emit(gg_v, gg_b.at[pick])
        send_v[...] = (dm_v[...] + norm_back(d_a, gain[0:1, :], hat, inv)).astype(BF)
        emit(send_v, send_h)
        for c in outs:
            c.wait()


def spec_any():
    return pl.BlockSpec(memory_space=pl.ANY)


def spec_vmem():
    return pl.BlockSpec(memory_space=pltpu.VMEM)


def forward_call(heads, slides, scal, ids, gain, fgain, head_w, known, label, count, x0, received, lm, wa, w1, w2, bufs):
    micro, tok, width = x0.shape
    ff = w1.shape[1]
    rows = known.shape[1]
    shapes = [
        ((tok, width), BF), ((tok, 3 * width), BF), ((heads, tok), F32), ((tok, width), BF),
        ((tok, width), F32), ((tok, ff), F32), ((tok, ff), BF), ((tok, width), BF), ((tok, width), BF),
        ((tok, width), F32), ((rows, width), BF), ((rows, LANES), BF), ((8, width), F32),
    ]
    fresh = bufs is None
    given = [] if fresh else list(bufs)
    vm = lambda index: pltpu.VMEM(*shapes[index])
    n_in = 14
    out = pl.pallas_call(
        functools.partial(forward_body, heads, slides, fresh),
        out_shape=[jax.ShapeDtypeStruct((tok, width), BF)]
        + [jax.ShapeDtypeStruct((micro,) + s, d) for s, d in shapes],
        in_specs=[pl.BlockSpec(memory_space=pltpu.SMEM)]
        + [spec_vmem()] * 6
        + [pl.BlockSpec(memory_space=pltpu.SMEM)]
        + [spec_any()] * (6 + len(given)),
        out_specs=[spec_any()] * (1 + len(shapes)),
        input_output_aliases={n_in + i: 1 + i for i in range(len(given))},
        scratch_shapes=[
            vm(0), pltpu.VMEM(lm.shape, F32), pltpu.VMEM(wa.shape, BF), pltpu.VMEM(w1.shape, BF),
            pltpu.VMEM(w2.shape, BF), vm(1), vm(2), vm(3), vm(4), vm(5), vm(6), vm(7), vm(8),
            pltpu.VMEM((tok, width), F32), vm(0),
            pltpu.VMEM((width, tok), BF), pltpu.VMEM((width, tok), BF), pltpu.VMEM((width, tok), F32),
            pltpu.VMEM((rows, width), F32), vm(10), vm(11), vm(12),
            pltpu.SemaphoreType.DMA((6,)), pltpu.SemaphoreType.DMA((10,)),
        ],
        compiler_params=pltpu.CompilerParams(vmem_limit_bytes=48 << 20),
        name="layer_forward",
    )(scal, ids, gain, fgain, head_w, known, label, count, x0, received, lm, wa, w1, w2, *given)
    return out[0], out[1:]


def backward_call(heads, scal, ids, gain, received, records, lm, wa, w1, w2, bufs):
    x_b, qkv_b, lse_b, mid_b, gp_b, dl_b = records
    micro, tok, width = x_b.shape
    ff = w1.shape[1]
    shapes = [((tok, width), BF), ((tok, ff), BF), ((tok, width), BF), ((tok, 3 * width), BF), ((8, width), F32)]
    fresh = bufs is None
    given = [] if fresh else list(bufs)
    n_in = 14
    out = pl.pallas_call(
        functools.partial(backward_body, heads, fresh),
        out_shape=[jax.ShapeDtypeStruct((tok, width), BF)]
        + [jax.ShapeDtypeStruct((micro,) + s, d) for s, d in shapes],
        in_specs=[pl.BlockSpec(memory_space=pltpu.SMEM)] + [spec_vmem()] * 2 + [spec_any()] * (11 + len(given)),
        out_specs=[spec_any()] * (1 + len(shapes)),
        input_output_aliases={n_in + i: 1 + i for i in range(len(given))},
        scratch_shapes=[
            pltpu.VMEM((tok, width), BF), pltpu.VMEM((tok, width), F32), pltpu.VMEM(lm.shape, F32),
            pltpu.VMEM(wa.shape, BF), pltpu.VMEM(w1.shape, BF), pltpu.VMEM(w2.shape, BF),
            pltpu.VMEM((tok, width), BF), pltpu.VMEM((tok, 3 * width), BF), pltpu.VMEM((heads, tok), F32),
            pltpu.VMEM((tok, width), F32), pltpu.VMEM((tok, ff), F32),
        ]
        + [pltpu.VMEM(s, d) for s, d in shapes]
        + [
            pltpu.VMEM((tok, width), BF), pltpu.VMEM((tok, width), F32),
            pltpu.VMEM((width, tok), BF), pltpu.VMEM((width, tok), BF),
            pltpu.VMEM((tok, width), BF), pltpu.VMEM((width, tok), BF), pltpu.VMEM((width, tok), F32),
            pltpu.VMEM((tok, 8 * tok), BF), pltpu.VMEM((tok, 8 * tok), BF),
            pltpu.SemaphoreType.DMA((11,)), pltpu.SemaphoreType.DMA((6,)),
        ],
        compiler_params=pltpu.CompilerParams(vmem_limit_bytes=48 << 20),
        name="layer_backward",
    )(scal, ids, gain, received, dl_b, lm, wa, w1, w2, x_b, qkv_b, lse_b, mid_b, gp_b, *given)
    return out[0], out[1:]


def forward_body(heads, slides, fresh, *refs):
    forward_kernel(heads, slides, *refs[:14], fresh, *refs[14:])


def backward_body(heads, fresh, *refs):
    backward_kernel(heads, *refs[:14], fresh, *refs[14:])


def adam(weight, grad, first, second, rate, decay):
    first = BETA_ONE * first + (1.0 - BETA_ONE) * grad
    second = BETA_TWO * second + (1.0 - BETA_TWO) * grad * grad
    mhat = first / (1.0 - BETA_ONE**STEP)
    vhat = second / (1.0 - BETA_TWO**STEP)
    return (first, second, weight - rate * (mhat / (jnp.sqrt(vhat) + ADAM_EPS) + decay * weight))


def per_device(
    tiles,
    slide_ids,
    coords,
    known,
    labels,
    mats,
    mats_m,
    mats_v,
    gains,
    gains_m,
    gains_v,
    final_gain,
    fgain_m,
    fgain_v,
    w_in,
    win_m,
    win_v,
    head,
    head_m,
    head_v,
):
    sections = lax.axis_size("section")
    section = lax.axis_index("section")
    first_dp = (lax.axis_index("dp") == 0).astype(jnp.float32)
    micro, tok = slide_ids.shape
    heads = HEADS
    slides, genes = known.shape[1:]
    wide = lax.all_gather(mats[0].astype(BF), "dp", axis=1, tiled=True)
    in_low = lax.all_gather(w_in.astype(BF), "section", axis=0, tiled=True)
    head_low = lax.all_gather(head.astype(BF), "section", axis=0, tiled=True)
    full_fgain = lax.all_gather(final_gain, "section", axis=0, tiled=True)
    gain = gains[0]
    width = wide.shape[1]
    known_f = known.astype(jnp.float32)
    labels_f = labels.astype(jnp.float32)
    count = jnp.maximum(lax.psum(jnp.sum(known_f), "dp"), 1.0)
    ticks = micro + sections - 1
    wa, w1, w2 = wide[0], wide[1], wide[2]
    lm = log_mult(heads, tok)
    pad = ((0, 0), (0, 16 - slides), (0, LANES - genes))
    known_p = jnp.pad(known_f, pad)
    labels_p = jnp.pad(labels_f, pad)
    head_p = jnp.pad(head_low, ((0, 0), (0, LANES - genes)))
    table = jax.vmap(lambda c: position_table(c, width), in_axes=1)(coords)
    x0 = (
        jnp.dot(tiles.reshape(micro * tok, -1), in_low, preferred_element_type=F32).reshape(
            micro, tok, width
        )
        + table
    ).astype(BF)

    def scalars(index):
        valid = (index >= 0) & (index < micro)
        return jnp.stack(
            [valid, jnp.clip(index, 0, micro - 1), section == 0, section == sections - 1]
        ).astype(jnp.int32)

    received = jnp.zeros((tok, width), BF)
    bufs = None
    for tick in range(ticks):
        send, bufs = forward_call(
            heads, slides, scalars(tick - section), slide_ids, gain, full_fgain[None, :], head_p,
            known_p, labels_p, count.reshape(1, 1), x0, received, lm, wa, w1, w2, bufs,
        )
        if tick + 1 < ticks:
            received = shifted(send, "section", 1)
    (x_b, qkv_b, lse_b, att_b, mid_b, gp_b, hid_b, a_b, b_b, dl_b, nl_b, dlog_b, side_b) = bufs
    records = (x_b, qkv_b, lse_b, mid_b, gp_b, dl_b)
    incoming = jnp.zeros((tok, width), BF)
    bufs = None
    sends = []
    for tick in range(ticks):
        send, bufs = backward_call(
            heads, scalars(tick - (sections - 1 - section)), slide_ids, gain, incoming, records,
            lm, wa, w1, w2, bufs,
        )
        sends.append(send)
        if tick + 1 < ticks:
            incoming = shifted(send, "section", -1)
    dbr_b, dup_b, dat_b, dqkv_b, gg_b = bufs
    flat = lambda v: v.reshape((-1, v.shape[-1]))
    grad_down = inner(flat(dbr_b), flat(hid_b)).astype(BF)
    grad_up = inner(flat(b_b), flat(dup_b)).astype(BF)
    grad_attn = jnp.concatenate(
        [inner(flat(a_b), flat(dqkv_b)).astype(BF), inner(flat(att_b), flat(dat_b)).astype(BF)], axis=1
    )
    grad_wide = jnp.stack([grad_attn, grad_up, grad_down])
    grad_gain = jnp.sum(gg_b, 0)[:2]
    on_first = section == 0
    on_last = section == sections - 1
    d_first = jnp.stack(sends[sections - 1 :])
    grad_in = inner(flat(tiles), flat(d_first))
    grad_in = jnp.where(on_first, grad_in, 0.0).astype(BF)
    grad_head = jnp.where(on_last, inner(flat(nl_b), flat(dlog_b)), 0.0)[:, :genes]
    side = jnp.where(on_last, jnp.sum(side_b, 0), 0.0)
    grad_fgain = side[0]
    loss_local = jnp.sum(side[1, :LANES])
    shard_wide = lax.psum_scatter(grad_wide, "dp", scatter_dimension=1, tiled=True).astype(F32)[None]
    part_in = lax.psum(
        lax.psum_scatter(grad_in, "section", scatter_dimension=0, tiled=True).astype(F32), "dp"
    )
    sum_gain, sum_head, sum_fgain = lax.psum((grad_gain, grad_head, grad_fgain), "dp")
    part_head, part_fgain = (
        lax.psum_scatter(sum_head, "section", scatter_dimension=0, tiled=True),
        lax.psum_scatter(sum_fgain, "section", scatter_dimension=0, tiled=True),
    )
    squares = jnp.sum(shard_wide * shard_wide) + first_dp * (
        jnp.sum(sum_gain * sum_gain)
        + jnp.sum(part_in * part_in)
        + jnp.sum(part_head * part_head)
        + jnp.sum(part_fgain * part_fgain)
    )
    total_sq, loss_sum = lax.psum((squares, loss_local), ("dp", "section"))
    grad_norm = jnp.sqrt(total_sq)
    factor = CLIP / jnp.maximum(grad_norm, CLIP)
    mats_out = adam(mats, shard_wide * factor, mats_m, mats_v, RATE, DECAY)
    gains_out = adam(gains, sum_gain[None] * factor, gains_m, gains_v, RATE_GAIN, 0.0)
    fgain_out = adam(final_gain, part_fgain * factor, fgain_m, fgain_v, RATE_GAIN, 0.0)
    in_out = adam(w_in, part_in * factor, win_m, win_v, RATE, DECAY)
    head_out = adam(head, part_head * factor, head_m, head_v, RATE, DECAY)
    return (
        grad_norm,
        loss_sum,
        count,
        mats_out[0],
        mats_out[1],
        mats_out[2],
        gains_out[0],
        gains_out[1],
        gains_out[2],
        fgain_out[0],
        fgain_out[1],
        fgain_out[2],
        in_out[0],
        in_out[1],
        in_out[2],
        head_out[0],
        head_out[1],
        head_out[2],
    )


def solution(mesh):
    placed = (
        P("dp", None, None),
        P("dp", None),
        P(None, "dp", None),
        P("dp", None, None),
        P("dp", None, None),
        P("section", None, "dp", None),
        P("section", None, "dp", None),
        P("section", None, "dp", None),
        P("section", None, None),
        P("section", None, None),
        P("section", None, None),
        P("section"),
        P("section"),
        P("section"),
        P("section", None),
        P("section", None),
        P("section", None),
        P("section", None),
        P("section", None),
        P("section", None),
    )
    return jax.shard_map(
        per_device,
        mesh=mesh,
        in_specs=placed,
        out_specs=(
            P(),
            P(),
            P(),
            P("section", None, "dp", None),
            P("section", None, "dp", None),
            P("section", None, "dp", None),
            P("section", None, None),
            P("section", None, None),
            P("section", None, None),
            P("section"),
            P("section"),
            P("section"),
            P("section", None),
            P("section", None),
            P("section", None),
            P("section", None),
            P("section", None),
            P("section", None),
        ),
        check_vma=False,
    )
```

time: 1670 us -> 971 us (0.58)
  matrix products: 444 us -> 18.2 us
  other arithmetic: 269 us -> 42.4 us
  waiting for transfers between devices: 562 us -> 400 us
  Pallas kernels: 0 us -> 122 us
  local copies, waits for them, and re-layouts: 201 us -> 140 us
  blocking collectives: 116 us -> 176 us
    dot_general x133 -> x1, matrix products: 289 us -> 4.34 us  [per_device(): jnp.dot(tiles.reshape(micro * tok, -1), in_low, preferred_element_type=F32)]
    reduce_scatter x1, waiting for transfers between devices: 402 us -> 148 us  [per_device(): lax.psum_scatter(grad_wide, 'dp', scatter_dimension=1, tiled=True)]
    dot_general x49 -> x6, matrix products: 155 us -> 13.8 us  [inner(): lax.dot_general(left, right, (((0,), (0,)), ((), ())), preferred_element_...]
    pallas_call x0 -> x14, Pallas kernels: none -> 122 us  [the longest x7 72 us: backward_call(): pl.pallas_call(functools.partial(backward_body, heads, fresh), out_shape=...]
    unnamed x1153 -> x310, local copies, waits for them, and re-layouts: 30.2 us -> 126 us
    add x18 -> x0, other arithmetic: 89.7 us -> none  [the longest x1 73.1 us: per_device(): grad_wide = grad_wide + use * g_wide]
    slice x57 -> x2, local copies, waits for them, and re-layouts: 80.9 us -> 0.02 us  [the longest x1 0.01 us: per_device(): grad_fgain = side[0]]
    ppermute x12, waiting for transfers between devices: 14.8 us -> 81.6 us  [shifted(): return lax.ppermute(block, axis, route)]
  transfers between devices with their start and end apart: 18 -> 17, of which waited for: 6 -> 14; matrix products, arithmetic and copies ran while one was open for 29% -> 6% of each run, Pallas kernels for 0% -> 2%
where the time goes in v1:
time: 971 us; the launch traced here: 960 us
  waiting for transfers between devices  400 us (41%)
  blocking collectives  176 us (18%)
  local copies, waits for them, and re-layouts  140 us (14%)
  Pallas kernels  122 us (13%)
  other arithmetic  42.4 us (4%)
  starting transfers between devices  37.7 us (4%)
  between operations  23.6 us (2%)
  matrix products  18.2 us (2%)
    all_gather x1, waiting for transfers between devices, per_device(): wide = lax.all_gather(mats[0].astype(BF), 'dp', axis=1, tiled=True)  171 us
    reduce_scatter x1, waiting for transfers between devices, per_device(): lax.psum_scatter(grad_wide, 'dp', scatter_dimension=1, tiled=True)  148 us
    unnamed x310, local copies, waits for them, and re-layouts  126 us
    psum x1, blocking collectives, per_device(): lax.psum((grad_gain, grad_head, grad_fgain), 'dp')  95.5 us
    ppermute x12, waiting for transfers between devices, shifted(): return lax.ppermute(block, axis, route)  81.6 us
    pallas_call x7, Pallas kernels, backward_call(): pl.pallas_call(functools.partial(backward_body, heads, fresh), out_shape=...  72 us
    pallas_call x7, Pallas kernels, forward_call(): pl.pallas_call(functools.partial(forward_body, heads, slides, fresh), out...  50.3 us
    psum x1, blocking collectives, per_device(): total_sq, loss_sum = lax.psum((squares, loss_local), ('dp', 'section'))  39.9 us
  transfers between devices with their start and end apart: 17, of which 14 were waited for; matrix products, arithmetic and copies ran while one was open for 6% of the time, Pallas kernels for 2%

profile of v1, /device:TPU:0, one launch (start us, length us, event | category | flops | bytes accessed | tf_op | source)
XLA Modules:
  0.0 960.0 jit_solution(8220524536548336224)
XLA Ops:
  13.8 23.7 %psum.49 = f32[]{:T(128)} all-reduce(f32[]{:T(128)} %fusion.27), channel_id=1, replica_groups=mesh['dp'=8,'section'=4] {'dp'}, use_global_device_ids=true, to_apply=%region_1.0 | all-reduce | flops 1 | bytes 8 | tf_op jit(solution)/shard_map/psum | solution.py:536
  39.0 5.6 all-reduce.3
  44.7 5.2 all-gather.1
  54.9 5.3 multiply_sine_fusion.1
  64.5 170.9 %all-gather.7.cloned.1.call-done = bf16[1,3,768,3072]{3,2,1,0:T(8,128)(2,1)} async-done(((bf16[1,3,96,3072]{3,2,1,0:T(8,128)(2,1)}), bf16[1,3,768,3072]{3,2,1,0:T(8,128)(2,1)}) %all-gather.7.cloned.1.call-update) | async-done | bytes 14155792 | tf_op jit(solution)/shard_map/all_gather | solution.py:528
  235.4 11.1 %slice_bitcast_fusion = (bf16[768,3072]{1,0:T(8,128)(2,1)}, bf16[768,3072]{1,0:T(8,128)(2,1)}, bf16[768,3072]{1,0:T(8,128)(2,1)}) fusion(bf16[1,3,768,3072]{3,2,1,0:T(8,128)(2,1)} %all-gather.7.cloned.1.call-done), kind=kLoop, calls=%fused_computation.5 | loop fusion | bytes 28311552 | tf_op jit(solution)/shard_map/squeeze | solution.py:538
  246.6 10.0 %layer_forward.7 = (bf16[128,768]{1,0:T(8,128)(2,1)}, bf16[4,128,768]{2,1,0:T(8,128)(2,1)S(1)}, bf16[4,128,2304]{2,1,0:T(8,128)(2,1)}, f32[4,16,128]{2,1,0:T(8,1...) custom-call(s32[4]{0:T(128)S(1)} %copy-done.122, ...), custom_call_target="tpu_custom_call" | custom-call | tf_op jit(solution)/shard_map/layer_forward/pallas_call | solution.py:425
  271.9 10.4 %layer_forward.8 = (bf16[128,768]{1,0:T(8,128)(2,1)}, bf16[4,128,768]{2,1,0:T(8,128)(2,1)S(1)}, bf16[4,128,2304]{2,1,0:T(8,128)(2,1)}, f32[4,16,128]{2,1,0:T(8,1...) custom-call(s32[4]{0:T(128)S(1)} %add_add_fusion.5.refs_0_, ...), custom_call_target="tpu_custom_call", output_to_operand_aliasing={{1}: (14, {}), {2}: (15, {}), {3}: (16, {}), {4}: (17, {}),... | custom-call | tf_op jit(solution)/shard_map/layer_forward/pallas_call | solution.py:425
  298.5 10.0 %layer_forward.9 = (bf16[128,768]{1,0:T(8,128)(2,1)}, bf16[4,128,768]{2,1,0:T(8,128)(2,1)S(1)}, bf16[4,128,2304]{2,1,0:T(8,128)(2,1)}, f32[4,16,128]{2,1,0:T(8,1...) custom-call(s32[4]{0:T(128)S(1)} %add_add_fusion.4.refs_0_, ...), custom_call_target="tpu_custom_call", output_to_operand_aliasing={{1}: (14, {}), {2}: (15, {}), {3}: (16, {}), {4}: (17, {}),... | custom-call | tf_op jit(solution)/shard_map/layer_forward/pallas_call | solution.py:425
  325.7 10.0 %layer_forward.10 = (bf16[128,768]{1,0:T(8,128)(2,1)}, bf16[4,128,768]{2,1,0:T(8,128)(2,1)S(1)}, bf16[4,128,2304]{2,1,0:T(8,128)(2,1)}, f32[4,16,128]{2,1,0:T(8,...) custom-call(s32[4]{0:T(128)S(1)} %add_add_fusion.3.refs_0_, ...), custom_call_target="tpu_custom_call", output_to_operand_aliasing={{1}: (14, {}), {2}: (15, {}), {3}: (16, {}), {4}: (17, {}),... | custom-call | tf_op jit(solution)/shard_map/layer_forward/pallas_call | solution.py:425
  339.7 6.4 collective-permute-start.3
  355.5 8.4 layer_forward.11
  367.9 8.7 collective-permute-start.4
  386.5 5.9 collective-permute-start.5
  402.8 5.9 layer_backward.7
  411.9 14.6 %collective-permute-done.6.refs_3_ = bf16[128,768]{1,0:T(8,128)(2,1)} collective-permute-done((bf16[128,768]{1,0:T(8,128)(2,1)}, bf16[128,768]{1,0:T(8,128)(2,1)}, u32[]{:S(2)}, u32[]{:S(2)}) %collective-permute-start.6) | collective-permute-done | bytes 196640 | tf_op jit(solution)/shard_map/ppermute | solution.py:27
  435.0 6.7 collective-permute-done.7.refs_3_
  446.3 6.2 layer_backward.9
  455.7 40.5 %collective-permute-done.8.refs_3_ = bf16[128,768]{1,0:T(8,128)(2,1)} collective-permute-done((bf16[128,768]{1,0:T(8,128)(2,1)}, bf16[128,768]{1,0:T(8,128)(2,1)}, u32[]{:S(2)}, u32[]{:S(2)}) %collective-permute-start.8) | collective-permute-done | bytes 196640 | tf_op jit(solution)/shard_map/ppermute | solution.py:27
  500.8 14.5 %layer_backward.10 = (bf16[128,768]{1,0:T(8,128)(2,1)S(1)}, bf16[4,128,768]{2,1,0:T(8,128)(2,1)S(1)}, bf16[4,128,3072]{2,1,0:T(8,128)(2,1)}, bf16[4,128,768]{2,1...) custom-call(s32[4]{0:T(128)S(1)} %add_add_fusion.10.refs_0_, ...), custom_call_target="tpu_custom_call", output_to_operand_aliasing={{1}: (14, {}), {2}: (15, {}), {3}: (16, {}), {4}: (17, {}),... | custom-call | tf_op jit(solution)/shard_map/layer_backward/pallas_call | solution.py:457
  516.7 5.5 collective-permute-done.9.refs_3_
  522.2 14.9 %layer_backward.11 = (bf16[128,768]{1,0:T(8,128)(2,1)S(1)}, bf16[4,128,768]{2,1,0:T(8,128)(2,1)S(1)}, bf16[4,128,3072]{2,1,0:T(8,128)(2,1)}, bf16[4,128,768]{2,1...) custom-call(s32[4]{0:T(128)S(1)} %add_add_fusion.9.refs_0_, ...), custom_call_target="tpu_custom_call", output_to_operand_aliasing={{1}: (14, {}), {2}: (15, {}), {3}: (16, {}), {4}: (17, {}),... | custom-call | tf_op jit(solution)/shard_map/layer_backward/pallas_call | solution.py:457
  538.8 5.3 collective-permute-done.10.refs_3_
  544.1 15.1 %layer_backward.12 = (bf16[128,768]{1,0:T(8,128)(2,1)}, bf16[4,128,768]{2,1,0:T(8,128)(2,1)S(1)}, bf16[4,128,3072]{2,1,0:T(8,128)(2,1)}, bf16[4,128,768]{2,1,0:T...) custom-call(s32[4]{0:T(128)S(1)} %add_add_fusion.8.refs_0_, ...), custom_call_target="tpu_custom_call", output_to_operand_aliasing={{1}: (14, {}), {2}: (15, {}), {3}: (16, {}), {4}: (17, {}),... | custom-call | tf_op jit(solution)/shard_map/layer_backward/pallas_call | solution.py:457
  563.4 5.0 collective-permute-done.11.refs_3_
  573.0 14.8 %layer_backward.13 = (bf16[128,768]{1,0:T(8,128)(2,1)S(1)}, bf16[4,128,768]{2,1,0:T(8,128)(2,1)S(1)}, bf16[4,128,3072]{2,1,0:T(8,128)(2,1)}, bf16[4,128,768]{2,1...) custom-call(s32[4]{0:T(128)S(1)} %add_add_fusion.7.refs_0_, ...), custom_call_target="tpu_custom_call", output_to_operand_aliasing={{1}: (14, {}), {2}: (15, {}), {3}: (16, {}), {4}: (17, {}),... | custom-call | tf_op jit(solution)/shard_map/layer_backward/pallas_call | solution.py:457
  611.0 6.4 pad_maximum_fusion
  623.4 5.8 all-reduce.4
  632.2 95.5 %all-reduce.8 = (f32[2,768]{1,0:T(2,128)S(1)}, f32[384,768]{0,1:T(8,128)S(1)}, f32[192,18]{0,1:T(8,128)S(1)}, f32[192]{0:T(256)S(1)}) all-reduce(f32[2,768]{1,0:T(2,128)S(1)} %slice.42, bf16[384,768]{0,1:T(8,128)(2,1)S(1)} %copy.218, f32[192,18]{0,1:T(8,128)S(1)} %copy.220, ...), channel_id=1, replica_groups=mesh['dp'=8,'section'=4] {'dp'}, use_global_device_ids=true, to_apply=%region_5.6 | all-reduce | flops 300096 | bytes 1810944 | tf_op jit(solution)/shard_map/psum | solution.py:602
  733.6 147.6 %reduce-scatter.8.cloned.1.call-done = bf16[3,96,3072]{2,1,0:T(8,128)(2,1)} async-done(((bf16[3,768,3072]{2,1,0:T(8,128)(2,1)}), bf16[3,96,3072]{2,1,0:T(8,128)(2,1)}) %reduce-scatter.8.cloned.1.call-update) | async-done | bytes 1769488 | tf_op jit(solution)/shard_map/reduce_scatter | solution.py:598
  887.5 39.9 %all-reduce.5 = (f32[]{:T(128)}, f32[]{:T(128)}) all-reduce(f32[]{:T(128)S(6)} %add.538, f32[]{:T(128)} %slice_reduce_fusion.1), channel_id=1, replica_groups=mesh['dp'=8,'section'=4] {'dp','section'}, use_global_device_ids=true, to_apply=%region_17.18 | all-reduce | flops 2 | bytes 16 | tf_op jit(solution)/shard_map/psum | solution.py:613
  942.6 8.0 multiply_subtract_fusion
  (405 shorter events, 192.4 us)
Async XLA Ops:
  7.2 53.0 %copy-start = (bf16[4,128,1536]{2,1,0:T(8,128)(2,1)S(1)}, bf16[4,128,1536]{2,1,0:T(8,128)(2,1)}, u32[]{:S(2)}) copy-start(bf16[4,128,1536]{2,1,0:T(8,128)(2,1)} %param.20) | copy-start | bytes 4718596
  7.2 53.0 %all-gather.5.cloned.1.call-start = ((), (), s32[]{:S(2)}) async-start(), calls=%async_computation.3 | async-start | bytes 2949120 | tf_op jit(solution)/shard_map/all_gather | solution.py:529
  9.5 28.0 %copy-start.145 = (u32[32]{0:T(128)S(1)}, u32[32]{0:T(128)}, u32[]{:S(2)}) copy-start(u32[32]{0:T(128)} %constant.209) | copy-start | bytes 388
  9.6 29.2 %copy-start.142 = (f32[192]{0:T(256)S(1)}, f32[192]{0:T(256)}, u32[]{:S(2)}) copy-start(f32[192]{0:T(256)} %param.31) | copy-start | bytes 2308
  9.6 35.1 %copy-start.134 = (f32[192,18]{0,1:T(8,128)S(1)}, f32[192,18]{0,1:T(8,128)}, u32[]{:S(2)}) copy-start(f32[192,18]{0,1:T(8,128)} %param.37) | copy-start | bytes 41476
  9.6 40.5 %copy-start.139 = (s32[4,3,18]{2,0,1:T(4,128)S(1)}, s32[4,3,18]{2,0,1:T(4,128)}, u32[]{:S(2)}) copy-start(s32[4,3,18]{2,0,1:T(4,128)} %param.24) | copy-start | bytes 2596
  9.6 225.8 %all-gather.7.cloned.1.call-start = ((), (), s32[]{:S(2)}) async-start(), calls=%async_computation.5 | async-start | bytes 15925248 | tf_op jit(solution)/shard_map/all_gather | solution.py:528
  13.1 40.3 %copy-start.144 = (s32[2,4,128]{2,1,0:T(4,128)S(1)}, s32[2,4,128]{2,1,0:T(4,128)}, u32[]{:S(2)}) copy-start(s32[2,4,128]{2,1,0:T(4,128)} %param.22) | copy-start | bytes 12292
  13.1 616.7 %reduce-scatter.12.cloned.1.call-start = ((), (), s32[]{:S(2)}) async-start(), calls=%async_computation.7 | async-start | bytes 491520
  54.8 338.6 %copy-start.3 = (f32[16,128,128]{2,1,0:T(8,128)}, f32[16,128,128]{2,1,0:T(8,128)S(1)}, u32[]{:S(2)}) copy-start(f32[16,128,128]{2,1,0:T(8,128)S(1)} %add_log_fusion.refs_10_.refs_5_) | copy-start | bytes 3145732
  64.5 182.0 %copy-start.108 = (f32[1,2,768]{2,1,0:T(2,128)S(1)}, f32[1,2,768]{2,1,0:T(2,128)}, u32[]{:S(2)}) copy-start(f32[1,2,768]{2,1,0:T(2,128)} %param.28) | copy-start | bytes 18436
  64.5 182.0 %copy-start.121 = (s32[4,128]{1,0:T(4,128)S(1)}, s32[4,128]{1,0:T(4,128)}, u32[]{:S(2)}) copy-start(s32[4,128]{1,0:T(4,128)} %refs_1_.27) | copy-start | bytes 6148
  260.6 2.7 collective-permute-start
  286.3 3.5 collective-permute-start.1
  312.5 4.7 collective-permute-start.2
  339.7 7.1 collective-permute-start.3
  367.9 9.4 collective-permute-start.4
  386.5 7.0 collective-permute-start.5
  402.8 23.7 %copy-start.2 = (f32[4,128,768]{2,1,0:T(8,128)S(1)}, f32[4,128,768]{2,1,0:T(8,128)}, u32[]{:S(2)}) copy-start(f32[4,128,768]{2,1,0:T(8,128)} %get-tuple-element.242.refs_4_) | copy-start | bytes 4718596
  410.5 16.0 %collective-permute-start.6 = (bf16[128,768]{1,0:T(8,128)(2,1)}, bf16[128,768]{1,0:T(8,128)(2,1)}, u32[]{:S(2)}, u32[]{:S(2)}) collective-permute-start(bf16[128,768]{1,0:T(8,128)(2,1)} %get-tuple-element.248), channel_id=1, source_target_pairs={{1,0},{2,1},{3,2},{5,4},{6,5},{7,6},{9,8},{10,9},{11,10},{13,12},{... | collective-permute-start | bytes 589832 | tf_op jit(solution)/shard_map/ppermute | solution.py:27
  433.6 8.0 collective-permute-start.7
  454.3 41.9 %collective-permute-start.8 = (bf16[128,768]{1,0:T(8,128)(2,1)}, bf16[128,768]{1,0:T(8,128)(2,1)}, u32[]{:S(2)}, u32[]{:S(2)}) collective-permute-start(bf16[128,768]{1,0:T(8,128)(2,1)} %get-tuple-element.260), channel_id=1, source_target_pairs={{1,0},{2,1},{3,2},{5,4},{6,5},{7,6},{9,8},{10,9},{11,10},{13,12},{... | collective-permute-start | bytes 589832 | tf_op jit(solution)/shard_map/ppermute | solution.py:27
  515.3 7.0 collective-permute-start.9
  522.2 16.3 %copy-start.120 = (bf16[4,16,128]{2,1,0:T(8,128)(2,1)S(1)}, bf16[4,16,128]{2,1,0:T(8,128)(2,1)}, u32[]{:S(2)}) copy-start(bf16[4,16,128]{2,1,0:T(8,128)(2,1)} %copy-done.119) | copy-start | bytes 49156
  537.1 22.1 %copy-start.125 = (bf16[128,768]{1,0:T(8,128)(2,1)}, bf16[128,768]{1,0:T(8,128)(2,1)S(1)}, u32[]{:S(2)}) copy-start(bf16[128,768]{1,0:T(8,128)(2,1)S(1)} %get-tuple-element.272) | copy-start | bytes 589828
  537.1 7.0 collective-permute-start.10
  561.0 7.3 collective-permute-start.11
  563.3 67.5 %reduce-scatter.10.cloned.1.call-start = ((), (), s32[]{:S(2)}) async-start(), calls=%async_computation.6 | async-start | bytes 2949120
  573.0 16.6 %copy-start.124 = (bf16[128,768]{1,0:T(8,128)(2,1)S(1)}, bf16[128,768]{1,0:T(8,128)(2,1)}, u32[]{:S(2)}) copy-start(bf16[128,768]{1,0:T(8,128)(2,1)} %copy-done.123) | copy-start | bytes 589828
  573.0 16.6 %copy-start.126 = (bf16[128,768]{1,0:T(8,128)(2,1)S(1)}, bf16[128,768]{1,0:T(8,128)(2,1)}, u32[]{:S(2)}) copy-start(bf16[128,768]{1,0:T(8,128)(2,1)} %copy-done.125) | copy-start | bytes 589828
  597.6 283.6 %reduce-scatter.8.cloned.1.call-start = ((), (), s32[]{:S(2)}) async-start(), calls=%async_computation.4 | async-start | bytes 15925248 | tf_op jit(solution)/shard_map/reduce_scatter | solution.py:598
  729.7 198.5 %copy-start.132 = (f32[384,768]{0,1:T(8,128)S(1)}, f32[384,768]{0,1:T(8,128)}, u32[]{:S(2)}) copy-start(f32[384,768]{0,1:T(8,128)} %copy.206) | copy-start | bytes 3538948
  (133 other events, 272.0 us)
Sparse Core Ops, SparseCore 0:
  10.2 26.7 all-gather.4
  39.7 195.6 all-gather.6
  563.4 23.9 reduce-scatter.11
  597.8 30.4 reduce-scatter.9
  632.2 248.9 reduce-scatter.7
